TPU v7x, 256 devices: a whole 4x4x8 slice. The times are simulated.
256 devices in a mesh: face: 8 (over x, core), patch: 32 (over y, z).
Axes of the slice: x: 4, y: 4, z: 8, core: 2. Of those that a mesh axis runs over, the one named last changes fastest.
Arguments:
- nodes: float32 [131072, 512], P(('face', 'patch')), may hold values from -6 to 6
- edges: bfloat16 [1048576, 512], P(('face', 'patch')), may hold values from -6 to 6
- sender: int32 [1048576], P(('face', 'patch')), may hold values from 0 to 8959, as said below
- receiver: int32 [1048576], P(('face', 'patch')), may hold values from 0 to 512, as said below
- send_rows: int32 [1024, 64], P(('face', 'patch')), may hold values from 0 to 511
- w_sender: bfloat16 [512, 512], replicated, may hold values from -0.25 to 0.25
- w_receiver: bfloat16 [512, 512], replicated, may hold values from -0.25 to 0.25
- w_edge: bfloat16 [512, 512], replicated, may hold values from -0.25 to 0.25
- bias_edge1: float32 [512], replicated, may hold values from -3 to 3
- w_edge2: bfloat16 [512, 512], replicated, may hold values from -0.25 to 0.25
- bias_edge2: float32 [512], replicated, may hold values from -3 to 3
- gain_edge: float32 [512], replicated, may hold values from 0.1 to 1.9
- shift_edge: float32 [512], replicated, may hold values from -3 to 3
- w_node_self: bfloat16 [512, 512], replicated, may hold values from -0.25 to 0.25
- w_node_aggr: bfloat16 [512, 512], replicated, may hold values from -0.25 to 0.25
- bias_node1: float32 [512], replicated, may hold values from -3 to 3
- w_node2: bfloat16 [512, 512], replicated, may hold values from -0.25 to 0.25
- bias_node2: float32 [512], replicated, may hold values from -3 to 3
- gain_node: float32 [512], replicated, may hold values from 0.1 to 1.9
- shift_node: float32 [512], replicated, may hold values from -3 to 3
Outputs:
- new_nodes: float32 [131072, 512], P(('face', 'patch'))
- new_edges: bfloat16 [1048576, 512], P(('face', 'patch'))
Inputs may be any that keep to these rules, and one draw needn't show every extreme that they name: `sender`: rows below 512 are the device's own nodes, the next 256 its halo, the rest the coarse rows. `receiver`: within each device's slots the receivers never fall; empty slots come last and carry 512.
All inputs are finite; a program needn't handle non-finite values.
Results may differ from a plain program's by a relative error of at most 0.0055.
Values may be sent and summed in bfloat16 or wider, within the bound.
No kernel may reach another device: no remote copies, remote signals or barrier semaphores. Data moves between devices by JAX's collectives and lax.ppermute only.
A program may use at most 128 MiB of HBM per device.

v0:
```python
import jax
import jax.numpy as jnp
from jax import lax
from jax.sharding import PartitionSpec as P

COARSE_DEV = 32


def shifted(block, axis, distance):
    devices = range(lax.axis_size(axis))
    route = [((i - distance) % len(devices), i) for i in devices]
    return lax.ppermute(block, axis, route)


def layer_norm(values, gain, shift):
    center = values - jnp.mean(values, axis=-1, keepdims=True)
    spread = jnp.mean(center * center, axis=-1, keepdims=True)
    return center * lax.rsqrt(spread + 1e-05) * gain + shift


def body(
    nodes,
    edges,
    sender,
    receiver,
    send_rows,
    w_sender,
    w_receiver,
    w_edge,
    bias_edge1,
    w_edge2,
    bias_edge2,
    gain_edge,
    shift_edge,
    w_node_self,
    w_node_aggr,
    bias_node1,
    w_node2,
    bias_node2,
    gain_node,
    shift_node,
):
    node_count = nodes.shape[0]
    coarse_count = COARSE_DEV
    own_bf = nodes.astype(jnp.bfloat16)
    beside_all = [shifted(own_bf[send_rows[k]], "patch", step) for k, step in ((0, 1), (1, -1))]
    across = [shifted(own_bf[send_rows[k]], "face", step) for k, step in ((2, 1), (3, -1))]
    coarse = lax.all_gather(own_bf[:coarse_count], ("face", "patch"), axis=0, tiled=True)
    table = jnp.concatenate([own_bf] + beside_all + across + [coarse], axis=0)
    sender_term = jnp.dot(table[sender], w_sender, preferred_element_type=jnp.float32)
    recv_term = jnp.dot(own_bf, w_receiver, preferred_element_type=jnp.float32)
    pre = sender_term + recv_term[jnp.minimum(receiver, node_count - 1)]
    pre = pre + jnp.dot(edges, w_edge, preferred_element_type=jnp.float32) + bias_edge1
    hidden = jax.nn.silu(pre).astype(jnp.bfloat16)
    update = layer_norm(
        jnp.dot(hidden, w_edge2, preferred_element_type=jnp.float32) + bias_edge2,
        gain_edge,
        shift_edge,
    )
    new_edges = (edges.astype(jnp.float32) + update).astype(jnp.bfloat16)
    targets = jnp.arange(node_count, dtype=jnp.int32)
    onehot = (receiver[None, :] == targets[:, None]).astype(jnp.bfloat16)
    aggregate = jnp.dot(
        onehot, update.astype(jnp.bfloat16), preferred_element_type=jnp.float32
    ).astype(jnp.bfloat16)
    inner = jnp.dot(own_bf, w_node_self, preferred_element_type=jnp.float32)
    inner = inner + jnp.dot(aggregate, w_node_aggr, preferred_element_type=jnp.float32) + bias_node1
    inner = jax.nn.silu(inner).astype(jnp.bfloat16)
    new_nodes = nodes + layer_norm(
        jnp.dot(inner, w_node2, preferred_element_type=jnp.float32) + bias_node2,
        gain_node,
        shift_node,
    )
    return (new_nodes, new_edges)


def solution(mesh):
    placed = (
        P(("face", "patch"), None),
        P(("face", "patch"), None),
        P(("face", "patch")),
        P(("face", "patch")),
        P(("face", "patch"), None),
        P(),
        P(),
        P(),
        P(),
        P(),
        P(),
        P(),
        P(),
        P(),
        P(),
        P(),
        P(),
        P(),
        P(),
        P(),
    )
    return jax.shard_map(
        body,
        mesh=mesh,
        in_specs=placed,
        out_specs=(P(("face", "patch"), None), P(("face", "patch"), None)),
        check_vma=False,
    )
```

profile of v0, /device:TPU:1, one launch (start us, length us, event | category | flops | bytes accessed | tf_op | source)
XLA Modules:
  0.0 210.6 jit_solution(7652141787721143915)
XLA Ops:
  7.2 0.0 copy-start
  7.2 0.0 copy-start.4
  7.2 0.0 all-gather.2.cloned.1.call-start
  7.2 2.2 %constant_dynamic-update-slice_fusion.5 = (bf16[8960,512]{1,0:T(8,128)(2,1)}, bf16[512,512]{1,0:T(8,128)(2,1)S(1)}) fusion(f32[512,512]{1,0:T(8,128)} %param.20), kind=kLoop, calls=%fused_computation.40 | loop fusion | flops 262143 | bytes 2097152
  9.4 0.6 slice.32
  10.0 0.0 all-gather.2.cloned.1.call-update
  10.1 0.8 fusion.21
  10.9 0.7 gather_fusion
  11.6 2.5 %collective-permute-start = (bf16[64,512]{1,0:T(8,128)(2,1)S(1)}, bf16[64,512]{1,0:T(8,128)(2,1)S(1)}, u32[]{:S(2)}, u32[]{:S(2)}) collective-permute-start(bf16[64,512]{1,0:T(8,128)(2,1)S(1)} %gather_fusion), channel_id=1, source_target_pairs={{31,0},{0,1},{1,2},{2,3},{3,4},{4,5},{5,6},{6,7},{7,8},{8,9},{9,10... | collective-permute-start | bytes 196616 | tf_op jit(solution)/shard_map/ppermute | solution.py:12
  14.2 0.7 gather_fusion.1
  14.9 6.5 %collective-permute-start.1 = (bf16[64,512]{1,0:T(8,128)(2,1)S(1)}, bf16[64,512]{1,0:T(8,128)(2,1)S(1)}, u32[]{:S(2)}, u32[]{:S(2)}) collective-permute-start(bf16[64,512]{1,0:T(8,128)(2,1)S(1)} %gather_fusion.1), channel_id=1, source_target_pairs={{1,0},{2,1},{3,2},{4,3},{5,4},{6,5},{7,6},{8,7},{9,8},{10,9},{11,1... | collective-permute-start | bytes 196616 | tf_op jit(solution)/shard_map/ppermute | solution.py:12
  21.4 1.3 gather_fusion.2
  22.7 2.1 collective-permute-start.2
  24.8 1.3 gather_fusion.3
  26.1 0.0 collective-permute-start.3
  26.1 1.5 fusion.26
  27.5 0.0 copy-start.5
  27.6 0.0 copy-start.6
  27.6 2.5 %fusion.25 = f32[512,512]{1,0:T(8,128)} fusion(bf16[512,512]{1,0:T(8,128)(2,1)S(1)} %get-tuple-element.5, bf16[512,512]{1,0:T(8,128)(2,1)} %param.33), kind=kOutput, calls=%fused_computation.59 | convolution fusion | flops 268435456 | bytes 2097152 | tf_op jit(solution)/shard_map/dot_general | solution.py:66
  30.0 0.0 copy-done.4
  30.0 7.8 %fusion.27 = f32[4096,512]{1,0:T(8,128)} fusion(bf16[4096,512]{1,0:T(8,128)(2,1)} %param.21, bf16[512,512]{1,0:T(8,128)(2,1)S(1)} %copy-done.4), kind=kOutput, calls=%fused_computation.61 | convolution fusion | flops 2147483648 | bytes 13107200 | tf_op jit(solution)/shard_map/dot_general | solution.py:53
  37.9 0.0 copy-done.5
  37.9 0.0 copy-done.6
  37.9 6.7 %copy.23 = bf16[4096,512]{0,1:T(8,128)(2,1)} copy(bf16[4096,512]{1,0:T(8,128)(2,1)} %param.21) | data formatting | bytes 8388608 | tf_op args[1]
  44.5 1.6 copy.22
  46.1 16.9 %gather_fusion.5 = f32[4096,512]{1,0:T(8,128)} fusion(f32[512,512]{1,0:T(8,128)S(1)} %fusion.26, s32[4096]{0:T(1024)S(1)} %get-tuple-element.15), kind=kCustom, calls=%fused_computation.5 | custom fusion | bytes 16793600 | tf_op jit(solution)/shard_map/gather | solution.py:52
  63.0 0.0 collective-permute-done
  63.0 0.6 constant_dynamic-update-slice_fusion.4
  63.6 0.0 collective-permute-done.1
  63.6 0.6 constant_dynamic-update-slice_fusion.3
  64.2 0.0 collective-permute-done.2
  64.2 0.6 constant_dynamic-update-slice_fusion.2
  64.9 0.0 collective-permute-done.3
  64.9 0.6 constant_dynamic-update-slice_fusion.1
  65.5 68.8 %all-gather.2.cloned.1.call-done = bf16[8192,512]{1,0:T(8,128)(2,1)} async-done(((bf16[32,512]{1,0:T(8,128)(2,1)}), bf16[8192,512]{1,0:T(8,128)(2,1)}) %all-gather.2.cloned.1.call-update) | async-done | bytes 8388624 | tf_op jit(solution)/shard_map/all_gather | solution.py:48
  134.3 7.2 %constant_dynamic-update-slice_fusion = bf16[8960,512]{1,0:T(8,128)(2,1)} fusion(bf16[8960,512]{1,0:T(8,128)(2,1)} %constant_dynamic-update-slice_fusion.1, bf16[8192,512]{1,0:T(8,128)(2,1)} %all-gather.2.cloned.1.call-done), kind=kLoop, calls=%fused_computation.35 | loop fusion | bytes 16777216 | tf_op jit(solution)/shard_map/concatenate | solution.py:49
  141.5 0.0 copy-start.7
  141.5 0.0 copy-start.13
  141.5 22.3 %gather_fusion.4 = bf16[4096,512]{1,0:T(8,128)(2,1)} fusion(bf16[8960,512]{1,0:T(8,128)(2,1)} %constant_dynamic-update-slice_fusion, s32[4096]{0:T(1024)S(1)} %get-tuple-element.14), kind=kCustom, calls=%fused_computation.4 | custom fusion | bytes 8404992 | tf_op jit(solution)/shard_map/gather | solution.py:50
  163.8 0.0 copy-done
  163.8 0.0 copy-done.7
  163.8 0.0 copy-done.12
  163.8 0.0 copy-done.13
  163.8 12.1 %add_reduce_fusion = (f32[4096]{0:T(1024)S(1)}, f32[4096,512]{0,1:T(8,128)}) fusion(f32[512]{0:T(512)S(1)} %copy-done.7, bf16[512,512]{1,0:T(8,128)(2,1)S(1)} %copy-done, f32[4096,512]{1,0:T(8,128)} %fusion.27, f32[4096,512]{1,0:T(8,128)} %gather_fusion.5, bf16[4096,512]{1,0:T(8,128)(2,1)} %gather_fusion.4, bf16[512,512]{1,0:T(8,128)(2,1)S(1)} %copy-done.12, ...), kind=kOutput, calls=%fused_computation.12 | convolution fusion | flops 4315934720 | bytes 30429184 | tf_op jit(solution)/shard_map/dot_general | solution.py:56
  175.9 0.0 copy-start.2
  176.0 0.0 copy-start.8
  176.0 4.9 %multiply_reduce_fusion = f32[4096]{0:T(1024)S(1)} fusion(f32[4096,512]{0,1:T(8,128)} %get-tuple-element.11, f32[4096]{0:T(1024)S(1)} %broadcast_multiply_fusion, f32[512]{0:T(512)S(1)} %copy-done.7), kind=kLoop, calls=%fused_computation.8 | loop fusion | flops 8384512 | bytes 8423424 | tf_op jit(solution)/shard_map/reduce_sum | solution.py:17
  180.9 0.8 copy-done.2
  181.7 0.0 copy-done.8
  181.7 0.0 copy-done.9
  181.7 4.2 %fusion.11 = bf16[512,512]{1,0:T(8,128)(2,1)} fusion(f32[4096,512]{0,1:T(8,128)S(1)} %copy-done.2, f32[512]{0:T(512)S(1)} %copy-done.8, f32[512]{0:T(512)S(1)} %copy-done.9, f32[4096]{0:T(1024)S(1)} %add_rsqrt_fusion, f32[4096]{0:T(1024)S(1)} %broadcast_multiply_fusion, f32[512]{0:T(512)S(1)} %copy-done.7, s32[4096]{0:T(1024)S(1)} %copy-done.6), kind=kOutput, calls=%fused_computation.24 | convolution fusion | flops 2162425856 | bytes 8968192 | tf_op jit(solution)/shard_map/dot_general | solution.py:63
  186.0 0.0 copy-done.3
  186.0 4.6 %add_convert_fusion = bf16[4096,512]{0,1:T(8,128)(2,1)} fusion(bf16[4096,512]{0,1:T(8,128)(2,1)S(1)} %copy-done.3, f32[4096,512]{0,1:T(8,128)S(1)} %copy-done.2, f32[512]{0:T(512)S(1)} %copy-done.8, f32[512]{0:T(512)S(1)} %copy-done.9, f32[4096]{0:T(1024)S(1)} %add_rsqrt_fusion, f32[4096]{0:T(1024)S(1)} %broadcast_multiply_fusion, f32[512]{0:T(512)S(1)} %copy-done.7), kind=kLoop, calls=%fused_computation.6 | loop fusion | flops 16777216 | bytes 16816128 | tf_op jit(solution)/shard_map/convert_element_type | solution.py:60
  190.6 0.0 copy-start.1
  190.6 6.5 %copy.25 = bf16[4096,512]{1,0:T(8,128)(2,1)} copy(bf16[4096,512]{0,1:T(8,128)(2,1)} %add_convert_fusion) | data formatting | bytes 8388608
  197.1 0.0 copy-done.14
  197.1 0.0 copy-done.15
  197.1 2.7 %fusion.24 = (f32[512]{0:T(512)S(1)}, f32[512,512]{0,1:T(8,128)S(1)}) fusion(f32[512]{0:T(512)S(1)} %copy-done.14, bf16[512,512]{1,0:T(8,128)(2,1)} %param.36, f32[512,512]{1,0:T(8,128)} %fusion.25, bf16[512,512]{1,0:T(8,128)(2,1)} %fusion.11, bf16[512,512]{1,0:T(8,128)(2,1)} %param.34, f32[512]{0:T(512)S(1)} %copy-done.15), kind=kOutput, calls=%fused_computation.58 | convolution fusion | flops 539229696 | bytes 3676160 | tf_op jit(solution)/shard_map/dot_general | solution.py:70
  199.8 0.2 multiply_reduce_fusion.1
  200.0 0.0 copy-done.10
  200.0 0.0 copy-done.11
  200.0 1.2 add_add_fusion
  201.2 2.5 %copy.24 = f32[512,512]{1,0:T(8,128)} copy(f32[512,512]{0,1:T(8,128)} %add_add_fusion) | data formatting | bytes 2097152
  203.7 0.0 copy-done.1
  (16 shorter events, 0.1 us)
Async XLA Ops:
  7.2 156.6 %copy-start = (bf16[512,512]{1,0:T(8,128)(2,1)S(1)}, bf16[512,512]{1,0:T(8,128)(2,1)}, u32[]{:S(2)}) copy-start(bf16[512,512]{1,0:T(8,128)(2,1)} %param.29) | copy-start | bytes 1572868
  7.2 22.9 %copy-start.4 = (bf16[512,512]{1,0:T(8,128)(2,1)S(1)}, bf16[512,512]{1,0:T(8,128)(2,1)}, u32[]{:S(2)}) copy-start(bf16[512,512]{1,0:T(8,128)(2,1)} %param.27) | copy-start | bytes 1572868
  7.2 127.1 %all-gather.2.cloned.1.call-start = ((), (), s32[]{:S(2)}) async-start(), calls=%async_computation | async-start | bytes 8421376 | tf_op jit(solution)/shard_map/all_gather | solution.py:48
  11.6 51.3 %collective-permute-start = (bf16[64,512]{1,0:T(8,128)(2,1)S(1)}, bf16[64,512]{1,0:T(8,128)(2,1)S(1)}, u32[]{:S(2)}, u32[]{:S(2)}) collective-permute-start(bf16[64,512]{1,0:T(8,128)(2,1)S(1)} %gather_fusion), channel_id=1, source_target_pairs={{31,0},{0,1},{1,2},{2,3},{3,4},{4,5},{5,6},{6,7},{7,8},{8,9},{9,10... | collective-permute-start | bytes 196616 | tf_op jit(solution)/shard_map/ppermute | solution.py:12
  14.9 48.7 %collective-permute-start.1 = (bf16[64,512]{1,0:T(8,128)(2,1)S(1)}, bf16[64,512]{1,0:T(8,128)(2,1)S(1)}, u32[]{:S(2)}, u32[]{:S(2)}) collective-permute-start(bf16[64,512]{1,0:T(8,128)(2,1)S(1)} %gather_fusion.1), channel_id=1, source_target_pairs={{1,0},{2,1},{3,2},{4,3},{5,4},{6,5},{7,6},{8,7},{9,8},{10,9},{11,1... | collective-permute-start | bytes 196616 | tf_op jit(solution)/shard_map/ppermute | solution.py:12
  22.7 41.5 %collective-permute-start.2 = (bf16[64,512]{1,0:T(8,128)(2,1)}, bf16[64,512]{1,0:T(8,128)(2,1)S(1)}, u32[]{:S(2)}, u32[]{:S(2)}) collective-permute-start(bf16[64,512]{1,0:T(8,128)(2,1)} %gather_fusion.2), channel_id=1, source_target_pairs={{224,0},{0,32},{32,64},{64,96},{96,128},{128,160},{160,192},{192,2... | collective-permute-start | bytes 196616 | tf_op jit(solution)/shard_map/ppermute | solution.py:12
  26.1 38.8 %collective-permute-start.3 = (bf16[64,512]{1,0:T(8,128)(2,1)}, bf16[64,512]{1,0:T(8,128)(2,1)S(1)}, u32[]{:S(2)}, u32[]{:S(2)}) collective-permute-start(bf16[64,512]{1,0:T(8,128)(2,1)} %gather_fusion.3), channel_id=1, source_target_pairs={{32,0},{64,32},{96,64},{128,96},{160,128},{192,160},{224,192},{0,2... | collective-permute-start | bytes 196616 | tf_op jit(solution)/shard_map/ppermute | solution.py:12
  27.5 10.3 %copy-start.5 = (s32[4096]{0:T(1024)S(1)}, s32[4096]{0:T(1024)}, u32[]{:S(2)}) copy-start(s32[4096]{0:T(1024)} %param.22) | copy-start | bytes 49156
  27.6 10.3 %copy-start.6 = (s32[4096]{0:T(1024)S(1)}, s32[4096]{0:T(1024)}, u32[]{:S(2)}) copy-start(s32[4096]{0:T(1024)} %param.23) | copy-start | bytes 49156
  141.5 22.3 %copy-start.7 = (f32[512]{0:T(512)S(1)}, f32[512]{0:T(512)}, u32[]{:S(2)}) copy-start(f32[512]{0:T(512)} %param.30) | copy-start | bytes 6148
  141.5 22.3 %copy-start.12 = (bf16[512,512]{1,0:T(8,128)(2,1)S(1)}, bf16[512,512]{1,0:T(8,128)(2,1)}, u32[]{:S(2)}) copy-start(bf16[512,512]{1,0:T(8,128)(2,1)} %param.25) | copy-start | bytes 1572868
  141.5 22.3 %copy-start.13 = (f32[512]{0:T(512)S(1)}, f32[512]{0:T(512)}, u32[]{:S(2)}) copy-start(f32[512]{0:T(512)} %param.28) | copy-start | bytes 6148
  175.9 5.8 %copy-start.2 = (f32[4096,512]{0,1:T(8,128)S(1)}, f32[4096,512]{0,1:T(8,128)}, u32[]{:S(2)}) copy-start(f32[4096,512]{0,1:T(8,128)} %get-tuple-element.11) | copy-start | bytes 25165828
  176.0 5.8 %copy-start.8 = (f32[512]{0:T(512)S(1)}, f32[512]{0:T(512)}, u32[]{:S(2)}) copy-start(f32[512]{0:T(512)} %param.32) | copy-start | bytes 6148
  176.0 5.8 %copy-start.9 = (f32[512]{0:T(512)S(1)}, f32[512]{0:T(512)}, u32[]{:S(2)}) copy-start(f32[512]{0:T(512)} %param.31) | copy-start | bytes 6148
  181.7 4.2 %copy-start.3 = (bf16[4096,512]{0,1:T(8,128)(2,1)S(1)}, bf16[4096,512]{0,1:T(8,128)(2,1)}, u32[]{:S(2)}) copy-start(bf16[4096,512]{0,1:T(8,128)(2,1)} %copy.23) | copy-start | bytes 12582916
  190.6 6.5 %copy-start.14 = (f32[512]{0:T(512)S(1)}, f32[512]{0:T(512)}, u32[]{:S(2)}) copy-start(f32[512]{0:T(512)} %param.37) | copy-start | bytes 6148
  190.6 6.5 %copy-start.15 = (f32[512]{0:T(512)S(1)}, f32[512]{0:T(512)}, u32[]{:S(2)}) copy-start(f32[512]{0:T(512)} %param.35) | copy-start | bytes 6148
  190.6 9.4 %copy-start.10 = (f32[512]{0:T(512)S(1)}, f32[512]{0:T(512)}, u32[]{:S(2)}) copy-start(f32[512]{0:T(512)} %param.39) | copy-start | bytes 6148
  190.6 9.4 %copy-start.11 = (f32[512]{0:T(512)S(1)}, f32[512]{0:T(512)}, u32[]{:S(2)}) copy-start(f32[512]{0:T(512)} %param.38) | copy-start | bytes 6148
  190.6 13.1 %copy-start.1 = (bf16[512,512]{1,0:T(8,128)(2,1)S(1)}, bf16[512,512]{1,0:T(8,128)(2,1)}, u32[]{:S(2)}) copy-start(bf16[512,512]{1,0:T(8,128)(2,1)} %param.29) | copy-start | bytes 1572868
Sparse Core Ops, SparseCore 0:
  11.7 122.4 all-gather.1
where the time goes:
time: 211 us
  local copies, waits for them, and re-layouts  71.7 us (34%)
  waiting for transfers between devices  68.8 us (33%)
  matrix products  30.8 us (15%)
  between operations  14.2 us (7%)
  other arithmetic  14 us (7%)
  starting transfers between devices  11.1 us (5%)
    all_gather x1, waiting for transfers between devices, body(): lax.all_gather(own_bf[:coarse_count], ('face', 'patch'), axis=0, tiled=True)  68.8 us
    gather x1, local copies, waits for them, and re-layouts, body(): table[sender]  22.3 us
    unnamed x40, local copies, waits for them, and re-layouts  20.7 us
    gather x1, local copies, waits for them, and re-layouts, body(): pre = sender_term + recv_term[jnp.minimum(receiver, node_count - 1)]  16.9 us
    dot_general x1, matrix products, body(): jnp.dot(hidden, w_edge2, preferred_element_type=jnp.float32) + bias_edge2  12.1 us
    ppermute x4, starting transfers between devices, shifted(): return lax.ppermute(block, axis, route)  11.1 us
    dot_general x1, matrix products, body(): jnp.dot(edges, w_edge, preferred_element_type=jnp.float32)  7.83 us
    concatenate x1, local copies, waits for them, and re-layouts, body(): table = jnp.concatenate([own_bf] + beside_all + across + [coarse], axis=0)  7.23 us
  transfers between devices with their start and end apart: 5, of which 1 were waited for; matrix products, arithmetic and copies ran while one was open for 21% of the time, Pallas kernels for 0%

commit v1 on v0

v1 whole, which is shorter than its diff:
```python
import numpy as np
import jax
import jax.numpy as jnp
from jax import lax
from jax.experimental import pallas as pl
from jax.experimental.pallas import tpu as pltpu
from jax.sharding import Mesh, PartitionSpec as P

AXES = ("x", "core", "y", "z")
SIZES = (4, 2, 4, 8)
NODE = 512
HALO = 64
NEAR = NODE + 4 * HALO
COARSE_DEV = 32
D = 512
EDGE = 4096
TILE = 512
TILES = EDGE // TILE
BLOCK = 256
BLOCKS = EDGE // BLOCK
F32 = jnp.float32
BF16 = jnp.bfloat16

STAGES = (
    (((0, 0, 4),) * 2, ((2, 2, 0),) * 2, ((2, 2, 4),) * 2),
    (((1, 1, 1),) * 2, ((-1, -1, -1),) * 2, ((0, 0, 2), (0, 0, -2))),
    (((-1, 1, 1), (1, -1, -1)),),
)
LAST = (((1, 0, 0), (-1, 0, 0)), ((0, 1, 0), (0, -1, 0)), ((0, 0, 1), (0, 0, -1)))


def places():
    own = np.zeros((2, 128), np.int32)
    for core in range(2):
        held = [(0, 0, 0)]
        for stage in STAGES + (LAST,):
            held = [
                ((a[0] + o[0]) % 4, (a[1] + o[1]) % 4, (a[2] + o[2]) % 8)
                for o in [(0, 0, 0)] + [pair[core] for pair in stage]
                for a in held
            ]
        assert len(set(held)) == 128
        for block, (x, y, z) in enumerate(held):
            own[core, x * 32 + y * 8 + z] = block
    return np.stack([np.stack([own[c] if c == k else 128 + own[k] for k in range(2)]) for c in range(2)])


PLACES = places()


def device(x, c, y, z):
    return ((x % 4) * 2 + c % 2) * 32 + (y % 4) * 8 + z % 8


def receive(block, source):
    spots = [(x, c, y, z) for x in range(4) for c in range(2) for y in range(4) for z in range(8)]
    return lax.ppermute(block, AXES, [(device(*source(*spot)), device(*spot)) for spot in spots])


def from_chip(block, pair):
    return receive(block, lambda x, c, y, z: (x + pair[c][0], c, y + pair[c][1], z + pair[c][2]))


def other_core(block):
    return receive(block, lambda x, c, y, z: (x, 1 - c, y, z))


def shift_patch(block, step):
    def source(x, c, y, z):
        j = (y * 8 + z - step) % 32
        return x, c, j // 8, j % 8

    return receive(block, source)


def shift_face(block, step):
    def source(x, c, y, z):
        f = (x * 2 + c - step) % 8
        return f // 2, f % 2, y, z

    return receive(block, source)


def dot(a, b):
    return jnp.dot(a, b, preferred_element_type=F32)


def dot_first(a, b):
    return lax.dot_general(a, b, (((0,), (0,)), ((), ())), preferred_element_type=F32)


def dot_last(a, b):
    return lax.dot_general(a, b, (((1,), (1,)), ((), ())), preferred_element_type=F32)


def silu(v):
    return v / (1.0 + jnp.exp(-v))


def layer_norm(v, gain, shift):
    center = v - jnp.mean(v, axis=-1, keepdims=True)
    spread = jnp.mean(center * center, axis=-1, keepdims=True)
    return center * lax.rsqrt(spread + 1e-05) * gain + shift


def iota(shape, dim):
    return lax.broadcasted_iota(jnp.int32, shape, dim)


def pick_kernel(nodes_ref, rows_ref, own_ref, out_ref):
    own = nodes_ref[...].astype(BF16)
    own_ref[...] = own
    hot = (iota((NODE, 4 * HALO), 0) == rows_ref[...]).astype(BF16)
    out_ref[...] = dot_first(hot, own).astype(BF16)


def near_kernel(
    snd_ref, rcv_ref, code_ref, edges_ref, own_ref, h0_ref, h1_ref, h2_ref, h3_ref,
    w_sender_ref, w_receiver_ref, w_edge_ref, b1_ref, w2_ref, b2_ref, gain_ref, shift_ref,
    new_edges_ref, agg_ref, slot_ref, info_ref, code_out_ref, rcv_out_ref, far_edges_ref, far_pre_ref,
    ts, tr, upper, far_edges, far_meta, pre_buf, count, sems,
):
    t = pl.program_id(0)

    @pl.when(t == 0)
    def _():
        w_sender = w_sender_ref[...]
        ts[:NODE] = dot(own_ref[...], w_sender).astype(BF16)
        for k, h_ref in enumerate((h0_ref, h1_ref, h2_ref, h3_ref)):
            ts[NODE + k * HALO:NODE + (k + 1) * HALO] = dot(h_ref[...], w_sender).astype(BF16)
        tr[...] = dot(own_ref[...], w_receiver_ref[...]).astype(BF16)
        upper[...] = (iota((TILE, TILE), 0) < iota((TILE, TILE), 1)).astype(BF16)
        far_edges[...] = jnp.zeros_like(far_edges)
        far_meta[...] = jnp.zeros_like(far_meta)
        agg_ref[...] = jnp.zeros_like(agg_ref)
        count[0] = 0

    snd = snd_ref[0]
    rcv = rcv_ref[0]
    code = code_ref[0]
    far = snd >= NEAR
    far_f = far.astype(F32)
    both = jnp.concatenate([snd, rcv, snd, rcv, snd, rcv, snd, rcv], axis=0)
    cols = jnp.transpose(both.astype(F32), (1, 0)).astype(jnp.int32)
    snd_c = cols[:, 0:1]
    rcv_c = jnp.minimum(cols[:, 1:2], NODE - 1)

    edges = edges_ref[...]
    hot_s = (iota((TILE, NEAR), 1) == snd_c).astype(BF16)
    hot_r = (iota((TILE, NODE), 1) == rcv_c).astype(BF16)
    pre = dot(edges, w_edge_ref[...]) + dot(hot_s, ts[...]) + dot(hot_r, tr[...]) + b1_ref[...]
    hidden = silu(pre).astype(BF16)
    update = layer_norm(dot(hidden, w2_ref[...]) + b2_ref[...], gain_ref[...], shift_ref[...])
    new = edges.astype(F32) + update
    new_edges_ref[...] = jnp.where(snd_c < NEAR, new, 0.0).astype(BF16)
    hot_n = (iota((NODE, TILE), 0) == jnp.where(far, -1, rcv)).astype(BF16)
    agg_ref[...] += dot(hot_n, update.astype(BF16))

    base = count[0]
    before = dot(jnp.broadcast_to(far_f, (8, TILE)).astype(BF16), upper[...])[0:1].astype(jnp.int32)
    number = jnp.sum(far_f).astype(jnp.int32)
    slot = jnp.where(far, base + before, -1)
    slot_ref[0] = slot
    info_ref[t] = base
    count[0] = base + number
    first = base // BLOCK
    last = jnp.where(number > 0, (base + number - 1) // BLOCK + 1, first)
    zero = jnp.zeros_like(code)
    meta = jnp.concatenate([code // 128, code % 128, rcv // 128, rcv % 128, zero, zero, zero, zero], axis=0)
    meta = meta.astype(F32).astype(BF16)

    def gather(b, carry):
        hot = (iota((BLOCK, TILE), 0) + b * BLOCK == slot).astype(BF16)
        rows = pl.ds(pl.multiple_of(b * BLOCK, BLOCK), BLOCK)
        far_edges[rows] = far_edges[rows] + dot(hot, edges).astype(BF16)
        far_meta[b] = far_meta[b] + dot_last(meta, hot)
        return carry

    lax.fori_loop(first, last, gather, 0)

    @pl.when(t == TILES - 1)
    def _():
        total = count[0]
        info_ref[TILES] = total

        def finish(b, carry):
            info = far_meta[b].astype(jnp.int32)
            code_b = info[0:1] * 128 + info[1:2]
            live = iota((1, BLOCK), 1) + b * BLOCK < total
            rcv_b = jnp.where(live, info[2:3] * 128 + info[3:4], NODE)
            code_out_ref[b] = code_b
            rcv_out_ref[b] = rcv_b
            return carry

        lax.fori_loop(0, BLOCKS, finish, 0)

        def push(b, carry):
            rows = pl.ds(pl.multiple_of(b * BLOCK, BLOCK), BLOCK)
            hot = (iota((NODE, BLOCK), 0) == jnp.minimum(rcv_out_ref[b], NODE - 1)).astype(BF16)
            pre_buf[...] = dot(far_edges[rows], w_edge_ref[...]) + dot_first(hot, tr[...]) + b1_ref[...]
            one = pltpu.make_async_copy(far_edges.at[rows], far_edges_ref.at[rows], sems.at[0])
            two = pltpu.make_async_copy(pre_buf, far_pre_ref.at[rows], sems.at[1])
            one.start()
            two.start()
            one.wait()
            two.wait()
            return carry

        lax.fori_loop(0, (total + BLOCK - 1) // BLOCK, push, 0)


def far_kernel(
    info_ref, code_ref, place_ref,
    *refs,
):
    pieces = refs[:8]
    (
        near_ref, slot_ref, rcv_ref, far_edges_ref, far_pre_ref, agg_ref, nodes_ref,
        w_sender_ref, w2_ref, b2_ref, gain_ref, shift_ref,
        w_self_ref, w_aggr_ref, bn1_ref, wn2_ref, bn2_ref, gain_n_ref, shift_n_ref,
        new_nodes_ref, new_edges_ref,
        table, rows_buf, edges_buf, pre_buf, new_far, agg, sems, row_sems,
    ) = refs[8:]
    t = pl.program_id(0)

    @pl.when(t == 0)
    def _():
        copies = [
            pltpu.make_async_copy(piece, table.at[k * 1024:(k + 1) * 1024], sems.at[k])
            for k, piece in enumerate(pieces)
        ]
        for copy in copies:
            copy.start()
        agg[...] = agg_ref[...]
        inner_self = dot(nodes_ref[...].astype(BF16), w_self_ref[...]) + bn1_ref[...]
        total = info_ref[TILES]
        for copy in copies:
            copy.wait()

        def block(b, carry):
            rows = pl.ds(pl.multiple_of(b * BLOCK, BLOCK), BLOCK)
            one = pltpu.make_async_copy(far_edges_ref.at[rows], edges_buf, row_sems.at[0])
            two = pltpu.make_async_copy(far_pre_ref.at[rows], pre_buf, row_sems.at[1])
            one.start()
            two.start()

            def gather(i, c):
                for k in range(8):
                    slot = i * 8 + k
                    code = code_ref[b * BLOCK + slot]
                    place = place_ref[code // 32] * 32 + code % 32
                    rows_buf[pl.ds(pl.multiple_of(slot * 4, 4), 4)] = table[place].astype(F32)
                return c

            lax.fori_loop(0, BLOCK // 8, gather, 0)
            sent = jnp.concatenate(
                [rows_buf[pl.ds(k, BLOCK, stride=4)] for k in range(4)], axis=1
            ).astype(BF16)
            one.wait()
            two.wait()
            pre = pre_buf[...] + dot(sent, w_sender_ref[...])
            hidden = silu(pre).astype(BF16)
            update = layer_norm(dot(hidden, w2_ref[...]) + b2_ref[...], gain_ref[...], shift_ref[...])
            new_far[rows] = (edges_buf[...].astype(F32) + update).astype(BF16)
            hot = (iota((NODE, BLOCK), 0) == rcv_ref[b]).astype(BF16)
            agg[...] += dot(hot, update.astype(BF16))
            return carry

        lax.fori_loop(0, (total + BLOCK - 1) // BLOCK, block, 0)
        aggregate = agg[...].astype(BF16)
        inner = silu(inner_self + dot(aggregate, w_aggr_ref[...])).astype(BF16)
        out = layer_norm(dot(inner, wn2_ref[...]) + bn2_ref[...], gain_n_ref[...], shift_n_ref[...])
        new_nodes_ref[...] = nodes_ref[...] + out

    base = info_ref[t]
    end = info_ref[t + 1]
    first = base // BLOCK
    last = jnp.where(end > base, (end - 1) // BLOCK + 1, first)
    new_edges_ref[...] = near_ref[...]

    def scatter(b, carry):
        hot = (iota((BLOCK, TILE), 0) + b * BLOCK == slot_ref[0]).astype(BF16)
        rows = pl.ds(pl.multiple_of(b * BLOCK, BLOCK), BLOCK)
        new_edges_ref[...] = new_edges_ref[...] + dot_first(hot, new_far[rows]).astype(BF16)
        return carry

    lax.fori_loop(first, last, scatter, 0)


def full(shape):
    return pl.BlockSpec(shape, lambda *_: (0,) * len(shape))


ANY = pl.BlockSpec(memory_space=pl.ANY)
SMEM = pl.BlockSpec(memory_space=pltpu.SMEM)
ROW = pl.BlockSpec((1, 1, TILE), lambda t: (t, 0, 0))
EDGES = pl.BlockSpec((TILE, D), lambda t: (t, 0))
SQUARE = full((D, D))
VECTOR = full((1, D))


def shape(dims, kind):
    return jax.ShapeDtypeStruct(dims, kind)


def pick(nodes, send_rows):
    return pl.pallas_call(
        pick_kernel,
        out_shape=(shape((NODE, D), BF16), shape((4 * HALO, D), BF16)),
        compiler_params=pltpu.CompilerParams(vmem_limit_bytes=16 << 20),
        cost_estimate=pl.CostEstimate(flops=2 * NODE * D * 256, bytes_accessed=2 << 20, transcendentals=0),
    )(nodes, send_rows.reshape(1, 4 * HALO))


def near(snd, rcv, code, edges, own, halo, w_sender, w_receiver, w_edge, b1, w2, b2, gain, shift):
    return pl.pallas_call(
        near_kernel,
        grid=(TILES,),
        in_specs=[ROW, ROW, ROW, EDGES, SQUARE] + [full((HALO, D))] * 4
        + [SQUARE, SQUARE, SQUARE, VECTOR, SQUARE, VECTOR, VECTOR, VECTOR],
        out_specs=[
            EDGES, SQUARE, ROW, SMEM, full((BLOCKS, 1, BLOCK)), full((BLOCKS, 1, BLOCK)), ANY, ANY,
        ],
        out_shape=(
            shape((EDGE, D), BF16), shape((NODE, D), F32), shape((TILES, 1, TILE), jnp.int32),
            shape((16,), jnp.int32),
            shape((BLOCKS, 1, BLOCK), jnp.int32), shape((BLOCKS, 1, BLOCK), jnp.int32),
            shape((EDGE, D), BF16), shape((EDGE, D), F32),
        ),
        scratch_shapes=[
            pltpu.VMEM((NEAR, D), BF16), pltpu.VMEM((NODE, D), BF16), pltpu.VMEM((TILE, TILE), BF16),
            pltpu.VMEM((EDGE, D), BF16), pltpu.VMEM((BLOCKS, 8, BLOCK), F32), pltpu.VMEM((BLOCK, D), F32),
            pltpu.SMEM((1,), jnp.int32), pltpu.SemaphoreType.DMA((2,)),
        ],
        compiler_params=pltpu.CompilerParams(vmem_limit_bytes=40 << 20),
        cost_estimate=pl.CostEstimate(flops=14 << 30, bytes_accessed=20 << 20, transcendentals=4 << 20),
    )(snd, rcv, code, edges, own, *halo, w_sender, w_receiver, w_edge, b1, w2, b2, gain, shift)


def far(info, code, place, pieces, near_edges, slot, rcv, far_edges, far_pre, agg, nodes, *weights):
    return pl.pallas_call(
        far_kernel,
        grid_spec=pltpu.PrefetchScalarGridSpec(
            num_scalar_prefetch=3,
            grid=(TILES,),
            in_specs=[ANY] * 8
            + [pl.BlockSpec((TILE, D), lambda t, *_: (t, 0)), pl.BlockSpec((1, 1, TILE), lambda t, *_: (t, 0, 0)),
               full((BLOCKS, 1, BLOCK)), ANY, ANY, SQUARE, SQUARE]
            + [SQUARE, SQUARE, VECTOR, VECTOR, VECTOR]
            + [SQUARE, SQUARE, VECTOR, SQUARE, VECTOR, VECTOR, VECTOR],
            out_specs=[SQUARE, pl.BlockSpec((TILE, D), lambda t, *_: (t, 0))],
            scratch_shapes=[
                pltpu.VMEM((8192, 4, 128), BF16), pltpu.VMEM((4 * BLOCK, 128), F32),
                pltpu.VMEM((BLOCK, D), BF16), pltpu.VMEM((BLOCK, D), F32), pltpu.VMEM((EDGE, D), BF16),
                pltpu.VMEM((NODE, D), F32), pltpu.SemaphoreType.DMA((8,)), pltpu.SemaphoreType.DMA((2,)),
            ],
        ),
        out_shape=(shape((NODE, D), F32), shape((EDGE, D), BF16)),
        input_output_aliases={11: 1},
        compiler_params=pltpu.CompilerParams(vmem_limit_bytes=48 << 20),
        cost_estimate=pl.CostEstimate(flops=4 << 30, bytes_accessed=24 << 20, transcendentals=1 << 20),
    )(info, code, place, *pieces, near_edges, slot, rcv, far_edges, far_pre, agg, nodes, *weights)


def body(
    nodes, edges, sender, receiver, send_rows,
    w_sender, w_receiver, w_edge, bias_edge1, w_edge2, bias_edge2, gain_edge, shift_edge,
    w_node_self, w_node_aggr, bias_node1, w_node2, bias_node2, gain_node, shift_node,
):
    row = lambda v: v.reshape(1, D)
    x, c, y, z = (lax.axis_index(a) for a in AXES)
    held = nodes[:COARSE_DEV].astype(BF16).reshape(COARSE_DEV, 4, 128)
    own, out = pick(nodes, send_rows)
    for stage in STAGES:
        held = jnp.concatenate([held] + [from_chip(held, pair) for pair in stage], axis=0)
    halo = [
        shift_patch(out[:HALO], 1), shift_patch(out[HALO:2 * HALO], -1),
        shift_face(out[2 * HALO:3 * HALO], 1), shift_face(out[3 * HALO:], -1),
    ]
    pieces = [held] + [from_chip(held, pair) for pair in LAST]
    pieces = pieces + [other_core(piece) for piece in pieces]

    q = jnp.maximum(sender - NEAR, 0)
    p, r = q // 32, q % 32
    d = ((p // 64 - x) % 4) * 32 + ((p // 8 - y) % 4) * 8 + (p - z) % 8
    code = (((p // 32) % 2) * 128 + d) * 32 + r
    place = lax.dynamic_index_in_dim(jnp.asarray(PLACES.reshape(2, 256)), c, keepdims=False)

    tiles = lambda v: v.reshape(TILES, 1, TILE)
    near_edges, agg, slot, info, far_code, far_rcv, far_edges, far_pre = near(
        tiles(sender), tiles(receiver), tiles(code), edges, own, halo,
        w_sender, w_receiver, w_edge, row(bias_edge1), w_edge2, row(bias_edge2), row(gain_edge), row(shift_edge),
    )
    return far(
        info, far_code.reshape(EDGE), place, pieces, near_edges, slot, far_rcv, far_edges, far_pre, agg, nodes,
        w_sender, w_edge2, row(bias_edge2), row(gain_edge), row(shift_edge),
        w_node_self, w_node_aggr, row(bias_node1), w_node2, row(bias_node2), row(gain_node), row(shift_node),
    )


def solution(mesh):
    grid = Mesh(mesh.devices.reshape(SIZES), AXES)
    split = P(AXES, None)
    return jax.shard_map(
        body,
        mesh=grid,
        in_specs=(split, split, P(AXES), P(AXES), split) + (P(),) * 15,
        out_specs=(split, split),
        check_vma=False,
    )
```

time: 211 us -> 145 us (0.69)
  local copies, waits for them, and re-layouts: 71.7 us -> 16.8 us
  Pallas kernels: 0 us -> 54 us
  waiting for transfers between devices: 68.8 us -> 35.1 us
  matrix products: 30.8 us -> 0 us
  starting transfers between devices: 11.1 us -> 36.4 us
  other arithmetic: 14 us -> 0.08 us
  between operations: 14.2 us -> 1.13 us
    all_gather x1 -> x0, waiting for transfers between devices: 68.8 us -> none  [body(): lax.all_gather(own_bf[:coarse_count], ('face', 'patch'), axis=0, tiled=True)]
    pallas_call x0 -> x3, Pallas kernels: none -> 54 us  [the longest x1 30.2 us: near(): pl.pallas_call(near_kernel, grid=(TILES,), in_specs=[ROW, ROW, ROW, EDGES...]
    gather x6 -> x0, local copies, waits for them, and re-layouts: 43.2 us -> none  [the longest x1 22.3 us: body(): table[sender]]
    ppermute x4 -> x18, waiting for transfers between devices: 0.01 us -> 35.1 us  [receive(): lax.ppermute(block, AXES, [(device(*source(*spot)), device(*spot)) for sp...]
    dot_general x6 -> x0, matrix products: 30.8 us -> none  [the longest x1 12.1 us: body(): jnp.dot(hidden, w_edge2, preferred_element_type=jnp.float32) + bias_edge2]
    ppermute x4 -> x18, starting transfers between devices: 11.1 us -> 36.4 us  [receive(): lax.ppermute(block, AXES, [(device(*source(*spot)), device(*spot)) for sp...]
    concatenate x1 -> x2, local copies, waits for them, and re-layouts: 7.23 us -> 0.32 us  [body(): jnp.concatenate([held] + [from_chip(held, pair) for pair in stage], axis=0)]
    unnamed x40 -> x66, local copies, waits for them, and re-layouts: 20.7 us -> 14.1 us
  transfers between devices with their start and end apart: 5 -> 18, of which waited for: 1 -> 6; matrix products, arithmetic and copies ran while one was open for 21% -> 1% of each run, Pallas kernels for 0% -> 21%
where the time goes in v1:
time: 145 us; the launch traced here: 144 us
  Pallas kernels  54 us (37%)
  starting transfers between devices  36.4 us (25%)
  waiting for transfers between devices  35.1 us (24%)
  local copies, waits for them, and re-layouts  16.8 us (12%)
    ppermute x18, starting transfers between devices, receive(): lax.ppermute(block, AXES, [(device(*source(*spot)), device(*spot)) for sp...  36.4 us
    ppermute x18, waiting for transfers between devices, receive(): lax.ppermute(block, AXES, [(device(*source(*spot)), device(*spot)) for sp...  35.1 us
    pallas_call x1, Pallas kernels, near(): pl.pallas_call(near_kernel, grid=(TILES,), in_specs=[ROW, ROW, ROW, EDGES...  30.2 us
    pallas_call x1, Pallas kernels, far(): pl.pallas_call(far_kernel, grid_spec=pltpu.PrefetchScalarGridSpec(num_sca...  23.5 us
    unnamed x66, local copies, waits for them, and re-layouts  14.1 us
  transfers between devices with their start and end apart: 18, of which 6 were waited for; matrix products, arithmetic and copies ran while one was open for 1% of the time, Pallas kernels for 21%

profile of v1, /device:TPU:1, one launch (start us, length us, event | category | flops | bytes accessed | tf_op | source)
XLA Modules:
  0.0 143.6 jit_solution(13140557772603969427)
XLA Ops:
  0.6 0.0 copy-start.29
  0.7 0.9 slice.23
  1.6 12.9 %collective-permute-start.6 = (bf16[32,4,128]{2,1,0:T(4,128)(2,1)S(1)}, bf16[32,4,128]{2,1,0:T(4,128)(2,1)S(1)}, u32[]{:S(2)}, u32[]{:S(2)}) collective-permute-start(bf16[32,4,128]{2,1,0:T(4,128)(2,1)S(1)} %reshape.58), channel_id=1, source_target_pairs={{148,0},{149,1},{150,2},{151,3},{144,4},{145,5},{146,6},{147,7},{1... | collective-permute-start | bytes 98312 | tf_op jit(solution)/shard_map/ppermute | solution.py:57
  14.6 0.0 collective-permute-start.5
  14.6 0.4 collective-permute-start.4
  15.0 6.6 %collective-permute-done.4 = bf16[32,4,128]{2,1,0:T(4,128)(2,1)S(1)} collective-permute-done((bf16[32,4,128]{2,1,0:T(4,128)(2,1)S(1)}, bf16[32,4,128]{2,1,0:T(4,128)(2,1)S(1)}, u32[]{:S(2)}, u32[]{:S(2)}) %collective-permute-start.4) | collective-permute-done | bytes 32800 | tf_op jit(solution)/shard_map/ppermute | solution.py:57
  21.6 0.0 collective-permute-done.5
  21.7 0.0 collective-permute-done.6
  21.7 4.2 %collective-permute-start.7 = (bf16[128,4,128]{2,1,0:T(4,128)(2,1)S(1)}, bf16[128,4,128]{2,1,0:T(4,128)(2,1)S(1)}, u32[]{:S(2)}, u32[]{:S(2)}) collective-permute-start(bf16[128,4,128]{2,1,0:T(4,128)(2,1)S(1)} %get-tuple-element.34), channel_id=1, source_target_pairs={{73,0},{74,1},{75,2},{76,3},{77,4},{78,5},{79,6},{72,7},{81,8},{82... | collective-permute-start | bytes 393224 | tf_op jit(solution)/shard_map/ppermute | solution.py:57
  25.9 0.0 collective-permute-start.8
  26.0 2.1 %collective-permute-start.9 = (bf16[128,4,128]{2,1,0:T(4,128)(2,1)S(1)}, bf16[128,4,128]{2,1,0:T(4,128)(2,1)S(1)}, u32[]{:S(2)}, u32[]{:S(2)}) collective-permute-start(bf16[128,4,128]{2,1,0:T(4,128)(2,1)S(1)} %get-tuple-element.34), channel_id=1, source_target_pairs={{2,0},{3,1},{4,2},{5,3},{6,4},{7,5},{0,6},{1,7},{10,8},{11,9},{12,... | collective-permute-start | bytes 393224 | tf_op jit(solution)/shard_map/ppermute | solution.py:57
  28.0 0.0 collective-permute-done.7
  28.0 0.1 constant_dynamic-update-slice_fusion.6
  28.1 7.0 %collective-permute-done.8 = bf16[128,4,128]{2,1,0:T(4,128)(2,1)S(1)} collective-permute-done((bf16[128,4,128]{2,1,0:T(4,128)(2,1)S(1)}, bf16[128,4,128]{2,1,0:T(4,128)(2,1)S(1)}, u32[]{:S(2)}, u32[]{:S(2)}) %collective-permute-start.8) | collective-permute-done | bytes 131104 | tf_op jit(solution)/shard_map/ppermute | solution.py:57
  35.2 0.1 constant_dynamic-update-slice_fusion.5
  35.3 0.0 collective-permute-done.9
  35.3 0.1 constant_dynamic-update-slice_fusion.4
  35.4 1.6 %collective-permute-start.10 = (bf16[512,4,128]{2,1,0:T(4,128)(2,1)S(1)}, bf16[512,4,128]{2,1,0:T(4,128)(2,1)S(1)}, u32[]{:S(2)}, u32[]{:S(2)}) collective-permute-start(bf16[512,4,128]{2,1,0:T(4,128)(2,1)S(1)} %get-tuple-element.26), channel_id=1, source_target_pairs={{201,0},{202,1},{203,2},{204,3},{205,4},{206,5},{207,6},{200,7},{2... | collective-permute-start | bytes 1572872 | tf_op jit(solution)/shard_map/ppermute | solution.py:57
  37.0 10.7 %collective-permute-done.10 = bf16[512,4,128]{2,1,0:T(4,128)(2,1)S(1)} collective-permute-done((bf16[512,4,128]{2,1,0:T(4,128)(2,1)S(1)}, bf16[512,4,128]{2,1,0:T(4,128)(2,1)S(1)}, u32[]{:S(2)}, u32[]{:S(2)}) %collective-permute-start.10) | collective-permute-done | bytes 524320 | tf_op jit(solution)/shard_map/ppermute | solution.py:57
  47.7 0.2 constant_dynamic-update-slice_fusion.11.refs_0_
  48.0 0.1 collective-permute-start.13
  48.1 0.1 collective-permute-start.12
  48.1 0.1 collective-permute-start.11
  48.2 0.8 reshape.52.rows_ref
  49.0 1.2 copy-done
  50.2 0.3 shard_map.212
  50.6 0.0 copy-start.21
  50.6 0.7 fusion.21
  51.3 0.1 copy-done.21
  51.4 10.5 %collective-permute-start.3 = (bf16[64,512]{1,0:T(8,128)(2,1)}, bf16[64,512]{1,0:T(8,128)(2,1)S(1)}, u32[]{:S(2)}, u32[]{:S(2)}) collective-permute-start(bf16[64,512]{1,0:T(8,128)(2,1)} %get-tuple-element.22), channel_id=1, source_target_pairs={{32,0},{33,1},{34,2},{35,3},{36,4},{37,5},{38,6},{39,7},{40,8},{41... | collective-permute-start | bytes 196616 | tf_op jit(solution)/shard_map/ppermute | solution.py:57
  61.9 0.0 collective-permute-start.2
  61.9 0.1 fusion.5
  61.9 8.8 %collective-permute-done.3.h3_ref = bf16[64,512]{1,0:T(8,128)(2,1)S(1)} collective-permute-done((bf16[64,512]{1,0:T(8,128)(2,1)}, bf16[64,512]{1,0:T(8,128)(2,1)S(1)}, u32[]{:S(2)}, u32[]{:S(2)}) %collective-permute-start.3) | collective-permute-done | bytes 65568 | tf_op jit(solution)/shard_map/ppermute | solution.py:57
  70.8 0.0 collective-permute-start.1
  70.8 1.5 %collective-permute-start = (bf16[64,512]{1,0:T(8,128)(2,1)S(1)}, bf16[64,512]{1,0:T(8,128)(2,1)S(1)}, u32[]{:S(2)}, u32[]{:S(2)}) collective-permute-start(bf16[64,512]{1,0:T(8,128)(2,1)S(1)} %get-tuple-element.25), channel_id=1, source_target_pairs={{31,0},{0,1},{1,2},{2,3},{3,4},{4,5},{5,6},{6,7},{7,8},{8,9},{9,10... | collective-permute-start | bytes 196616 | tf_op jit(solution)/shard_map/ppermute | solution.py:57
  72.2 1.6 %collective-permute-done.1.h1_ref = bf16[64,512]{1,0:T(8,128)(2,1)S(1)} collective-permute-done((bf16[64,512]{1,0:T(8,128)(2,1)S(1)}, bf16[64,512]{1,0:T(8,128)(2,1)S(1)}, u32[]{:S(2)}, u32[]{:S(2)}) %collective-permute-start.1) | collective-permute-done | bytes 65568 | tf_op jit(solution)/shard_map/ppermute | solution.py:57
  73.9 2.2 %collective-permute-start.14 = (bf16[1024,4,128]{2,1,0:T(4,128)(2,1)S(1)}, bf16[1024,4,128]{2,1,0:T(4,128)(2,1)S(1)}, u32[]{:S(2)}, u32[]{:S(2)}) collective-permute-start(bf16[1024,4,128]{2,1,0:T(4,128)(2,1)S(1)} %constant_dynamic-update-slice_fusion.11.refs_0_), channel_id=1, source_target_pairs={{32,0},{33,1},{34,2},{35,3},{36,4},{37,5},{38,6},{39,7},{40,8},{41... | collective-permute-start | bytes 3145736 | tf_op jit(solution)/shard_map/ppermute | solution.py:57
  76.1 0.0 collective-permute-done.13.refs_3_
  76.1 0.0 collective-permute-start.17
  76.1 0.5 collective-permute-start.16
  76.6 0.0 collective-permute-done.11.refs_1_
  76.6 0.3 collective-permute-start.15
  76.9 0.3 collective-permute-done.h0_ref
  77.2 0.0 copy-start.3
  77.2 1.0 copy-done.3
  78.3 1.0 copy-done.5
  79.3 2.2 %copy-done.18 = bf16[4096,512]{1,0:T(8,128)(2,1)S(1)} copy-done((bf16[4096,512]{1,0:T(8,128)(2,1)S(1)}, bf16[4096,512]{1,0:T(8,128)(2,1)}, u32[]{:S(2)}) %copy-start.18) | copy-done | bytes 4194328
  81.5 1.0 copy-done.19
  82.6 1.0 copy-done.20
  83.6 1.0 copy-done.22
  84.6 0.0 copy-start.9
  84.7 0.0 copy-start.14
  84.7 0.0 copy-start.15
  84.7 0.0 copy-start.16
  84.7 0.0 copy-start.17
  84.7 30.2 %shard_map.213 = (bf16[4096,512]{1,0:T(8,128)(2,1)}, f32[512,512]{1,0:T(8,128)S(1)}, s32[8,1,512]{2,1,0:T(1,128)S(1)}, s32[16]{0:T(128)S(1)}, s32[16,1,256]{2,1,...) custom-call(s32[8,1,512]{2,1,0:T(1,128)S(1)} %bitcast.14, ...), custom_call_target="tpu_custom_call" | custom-call | flops 15032385536 | bytes 20971520 | tf_op jit(solution)/shard_map/pallas_call | solution.py:316
  115.0 2.1 %copy-done.1 = bf16[4096,512]{1,0:T(8,128)(2,1)} copy-done((bf16[4096,512]{1,0:T(8,128)(2,1)}, bf16[4096,512]{1,0:T(8,128)(2,1)S(1)}, u32[]{:S(2)}) %copy-start.1) | copy-done | bytes 4194328
  117.0 1.0 copy-done.2
  118.0 0.0 collective-permute-done.16.refs_6_
  118.0 0.9 copy-done.25
  119.0 0.4 copy-done.26
  119.3 0.3 copy-done.27
  119.6 0.3 copy-done.28
  120.0 23.5 %shard_map.214 = (f32[512,512]{1,0:T(8,128)}, bf16[4096,512]{1,0:T(8,128)(2,1)}) custom-call(s32[16]{0:T(128)S(1)} %get-tuple-element.14.info_ref, s32[4096]{0:T(1024)S(1)} %bitcast.13, s32[256]{0:T(256)S(1)} %bitcast.16, bf16[1024,4,128]{2,1,0:T(4,128)(2,1)S(1)} %constant_dynamic-update-slice_fusion.11.refs_0_, ...), custom_call_target="tpu_custom_call", output_to_operand_aliasing={{1}: (11, {})} | custom-call | flops 4294967296 | bytes 25165824 | tf_op jit(solution)/shard_map/pallas_call | solution.py:341
  (49 shorter events, 0.3 us)
Async XLA Ops:
  0.6 71.6 %copy-start.29 = (s32[2,256]{1,0:T(2,128)S(1)}, s32[2,256]{1,0:T(2,128)}, u32[]{:S(2)}) copy-start(s32[2,256]{1,0:T(2,128)} %constant.126.clone) | copy-start | bytes 6148
  0.6 61.2 %copy-start.10 = (s32[4096]{0:T(1024)S(1)}, s32[4096]{0:T(1024)}, u32[]{:S(2)}) copy-start(s32[4096]{0:T(1024)} %param.23) | copy-start | bytes 49156
  0.7 76.5 %copy-start.13 = (f32[512]{0:T(512)S(1)}, f32[512]{0:T(512)}, u32[]{:S(2)}) copy-start(f32[512]{0:T(512)} %param.33) | copy-start | bytes 6148
  0.7 76.5 %copy-start.12 = (f32[512]{0:T(512)S(1)}, f32[512]{0:T(512)}, u32[]{:S(2)}) copy-start(f32[512]{0:T(512)} %param.32) | copy-start | bytes 6148
  0.7 76.5 %copy-start.11 = (f32[512]{0:T(512)S(1)}, f32[512]{0:T(512)}, u32[]{:S(2)}) copy-start(f32[512]{0:T(512)} %param.31) | copy-start | bytes 6148
  0.7 76.5 %copy-start.24 = (f32[512]{0:T(512)S(1)}, f32[512]{0:T(512)}, u32[]{:S(2)}) copy-start(f32[512]{0:T(512)} %param.29) | copy-start | bytes 6148
  0.7 76.5 %copy-start.23 = (s32[4096]{0:T(1024)S(1)}, s32[4096]{0:T(1024)}, u32[]{:S(2)}) copy-start(s32[4096]{0:T(1024)} %param.24) | copy-start | bytes 49156
  1.6 20.0 %collective-permute-start.6 = (bf16[32,4,128]{2,1,0:T(4,128)(2,1)S(1)}, bf16[32,4,128]{2,1,0:T(4,128)(2,1)S(1)}, u32[]{:S(2)}, u32[]{:S(2)}) collective-permute-start(bf16[32,4,128]{2,1,0:T(4,128)(2,1)S(1)} %reshape.58), channel_id=1, source_target_pairs={{148,0},{149,1},{150,2},{151,3},{144,4},{145,5},{146,6},{147,7},{1... | collective-permute-start | bytes 98312 | tf_op jit(solution)/shard_map/ppermute | solution.py:57
  14.6 7.1 %collective-permute-start.5 = (bf16[32,4,128]{2,1,0:T(4,128)(2,1)S(1)}, bf16[32,4,128]{2,1,0:T(4,128)(2,1)S(1)}, u32[]{:S(2)}, u32[]{:S(2)}) collective-permute-start(bf16[32,4,128]{2,1,0:T(4,128)(2,1)S(1)} %reshape.58), channel_id=1, source_target_pairs={{144,0},{145,1},{146,2},{147,3},{148,4},{149,5},{150,6},{151,7},{1... | collective-permute-start | bytes 98312 | tf_op jit(solution)/shard_map/ppermute | solution.py:57
  14.6 7.0 %collective-permute-start.4 = (bf16[32,4,128]{2,1,0:T(4,128)(2,1)S(1)}, bf16[32,4,128]{2,1,0:T(4,128)(2,1)S(1)}, u32[]{:S(2)}, u32[]{:S(2)}) collective-permute-start(bf16[32,4,128]{2,1,0:T(4,128)(2,1)S(1)} %reshape.58), channel_id=1, source_target_pairs={{4,0},{5,1},{6,2},{7,3},{0,4},{1,5},{2,6},{3,7},{12,8},{13,9},{14,... | collective-permute-start | bytes 98312 | tf_op jit(solution)/shard_map/ppermute | solution.py:57
  21.7 6.3 %collective-permute-start.7 = (bf16[128,4,128]{2,1,0:T(4,128)(2,1)S(1)}, bf16[128,4,128]{2,1,0:T(4,128)(2,1)S(1)}, u32[]{:S(2)}, u32[]{:S(2)}) collective-permute-start(bf16[128,4,128]{2,1,0:T(4,128)(2,1)S(1)} %get-tuple-element.34), channel_id=1, source_target_pairs={{73,0},{74,1},{75,2},{76,3},{77,4},{78,5},{79,6},{72,7},{81,8},{82... | collective-permute-start | bytes 393224 | tf_op jit(solution)/shard_map/ppermute | solution.py:57
  25.9 9.2 %collective-permute-start.8 = (bf16[128,4,128]{2,1,0:T(4,128)(2,1)S(1)}, bf16[128,4,128]{2,1,0:T(4,128)(2,1)S(1)}, u32[]{:S(2)}, u32[]{:S(2)}) collective-permute-start(bf16[128,4,128]{2,1,0:T(4,128)(2,1)S(1)} %get-tuple-element.34), channel_id=1, source_target_pairs={{223,0},{216,1},{217,2},{218,3},{219,4},{220,5},{221,6},{222,7},{1... | collective-permute-start | bytes 393224 | tf_op jit(solution)/shard_map/ppermute | solution.py:57
  26.0 9.3 %collective-permute-start.9 = (bf16[128,4,128]{2,1,0:T(4,128)(2,1)S(1)}, bf16[128,4,128]{2,1,0:T(4,128)(2,1)S(1)}, u32[]{:S(2)}, u32[]{:S(2)}) collective-permute-start(bf16[128,4,128]{2,1,0:T(4,128)(2,1)S(1)} %get-tuple-element.34), channel_id=1, source_target_pairs={{2,0},{3,1},{4,2},{5,3},{6,4},{7,5},{0,6},{1,7},{10,8},{11,9},{12,... | collective-permute-start | bytes 393224 | tf_op jit(solution)/shard_map/ppermute | solution.py:57
  35.4 12.3 %collective-permute-start.10 = (bf16[512,4,128]{2,1,0:T(4,128)(2,1)S(1)}, bf16[512,4,128]{2,1,0:T(4,128)(2,1)S(1)}, u32[]{:S(2)}, u32[]{:S(2)}) collective-permute-start(bf16[512,4,128]{2,1,0:T(4,128)(2,1)S(1)} %get-tuple-element.26), channel_id=1, source_target_pairs={{201,0},{202,1},{203,2},{204,3},{205,4},{206,5},{207,6},{200,7},{2... | collective-permute-start | bytes 1572872 | tf_op jit(solution)/shard_map/ppermute | solution.py:57
  48.0 28.1 %collective-permute-start.13 = (bf16[1024,4,128]{2,1,0:T(4,128)(2,1)S(1)}, bf16[1024,4,128]{2,1,0:T(4,128)(2,1)}, u32[]{:S(2)}, u32[]{:S(2)}) collective-permute-start(bf16[1024,4,128]{2,1,0:T(4,128)(2,1)S(1)} %constant_dynamic-update-slice_fusion.11.refs_0_), channel_id=1, source_target_pairs={{1,0},{2,1},{3,2},{4,3},{5,4},{6,5},{7,6},{0,7},{9,8},{10,9},{11,1... | collective-permute-start | bytes 3145736 | tf_op jit(solution)/shard_map/ppermute | solution.py:57
  48.1 28.1 %collective-permute-start.12 = (bf16[1024,4,128]{2,1,0:T(4,128)(2,1)S(1)}, bf16[1024,4,128]{2,1,0:T(4,128)(2,1)S(1)}, u32[]{:S(2)}, u32[]{:S(2)}) collective-permute-start(bf16[1024,4,128]{2,1,0:T(4,128)(2,1)S(1)} %constant_dynamic-update-slice_fusion.11.refs_0_), channel_id=1, source_target_pairs={{8,0},{9,1},{10,2},{11,3},{12,4},{13,5},{14,6},{15,7},{16,8},{17,9... | collective-permute-start | bytes 3145736 | tf_op jit(solution)/shard_map/ppermute | solution.py:57
  48.1 28.5 %collective-permute-start.11 = (bf16[1024,4,128]{2,1,0:T(4,128)(2,1)S(1)}, bf16[1024,4,128]{2,1,0:T(4,128)(2,1)S(1)}, u32[]{:S(2)}, u32[]{:S(2)}) collective-permute-start(bf16[1024,4,128]{2,1,0:T(4,128)(2,1)S(1)} %constant_dynamic-update-slice_fusion.11.refs_0_), channel_id=1, source_target_pairs={{64,0},{65,1},{66,2},{67,3},{68,4},{69,5},{70,6},{71,7},{72,8},{73... | collective-permute-start | bytes 3145736 | tf_op jit(solution)/shard_map/ppermute | solution.py:57
  49.0 1.2 copy-start
  50.6 0.8 copy-start.21
  51.4 19.4 %collective-permute-start.3 = (bf16[64,512]{1,0:T(8,128)(2,1)}, bf16[64,512]{1,0:T(8,128)(2,1)S(1)}, u32[]{:S(2)}, u32[]{:S(2)}) collective-permute-start(bf16[64,512]{1,0:T(8,128)(2,1)} %get-tuple-element.22), channel_id=1, source_target_pairs={{32,0},{33,1},{34,2},{35,3},{36,4},{37,5},{38,6},{39,7},{40,8},{41... | collective-permute-start | bytes 196616 | tf_op jit(solution)/shard_map/ppermute | solution.py:57
  61.9 8.9 %collective-permute-start.2 = (bf16[64,512]{1,0:T(8,128)(2,1)S(1)}, bf16[64,512]{1,0:T(8,128)(2,1)S(1)}, u32[]{:S(2)}, u32[]{:S(2)}) collective-permute-start(bf16[64,512]{1,0:T(8,128)(2,1)S(1)} %get-tuple-element.23), channel_id=1, source_target_pairs={{224,0},{225,1},{226,2},{227,3},{228,4},{229,5},{230,6},{231,7},{2... | collective-permute-start | bytes 196616 | tf_op jit(solution)/shard_map/ppermute | solution.py:57
  70.8 3.1 %collective-permute-start.1 = (bf16[64,512]{1,0:T(8,128)(2,1)S(1)}, bf16[64,512]{1,0:T(8,128)(2,1)S(1)}, u32[]{:S(2)}, u32[]{:S(2)}) collective-permute-start(bf16[64,512]{1,0:T(8,128)(2,1)S(1)} %get-tuple-element.24), channel_id=1, source_target_pairs={{1,0},{2,1},{3,2},{4,3},{5,4},{6,5},{7,6},{8,7},{9,8},{10,9},{11,1... | collective-permute-start | bytes 196616 | tf_op jit(solution)/shard_map/ppermute | solution.py:57
  70.8 6.4 %collective-permute-start = (bf16[64,512]{1,0:T(8,128)(2,1)S(1)}, bf16[64,512]{1,0:T(8,128)(2,1)S(1)}, u32[]{:S(2)}, u32[]{:S(2)}) collective-permute-start(bf16[64,512]{1,0:T(8,128)(2,1)S(1)} %get-tuple-element.25), channel_id=1, source_target_pairs={{31,0},{0,1},{1,2},{2,3},{3,4},{4,5},{5,6},{6,7},{7,8},{8,9},{9,10... | collective-permute-start | bytes 196616 | tf_op jit(solution)/shard_map/ppermute | solution.py:57
  73.9 44.1 %collective-permute-start.14 = (bf16[1024,4,128]{2,1,0:T(4,128)(2,1)S(1)}, bf16[1024,4,128]{2,1,0:T(4,128)(2,1)S(1)}, u32[]{:S(2)}, u32[]{:S(2)}) collective-permute-start(bf16[1024,4,128]{2,1,0:T(4,128)(2,1)S(1)} %constant_dynamic-update-slice_fusion.11.refs_0_), channel_id=1, source_target_pairs={{32,0},{33,1},{34,2},{35,3},{36,4},{37,5},{38,6},{39,7},{40,8},{41... | collective-permute-start | bytes 3145736 | tf_op jit(solution)/shard_map/ppermute | solution.py:57
  76.1 41.9 %collective-permute-start.17 = (bf16[1024,4,128]{2,1,0:T(4,128)(2,1)}, bf16[1024,4,128]{2,1,0:T(4,128)(2,1)S(1)}, u32[]{:S(2)}, u32[]{:S(2)}) collective-permute-start(bf16[1024,4,128]{2,1,0:T(4,128)(2,1)} %collective-permute-done.13.refs_3_), channel_id=1, source_target_pairs={{32,0},{33,1},{34,2},{35,3},{36,4},{37,5},{38,6},{39,7},{40,8},{41... | collective-permute-start | bytes 3145736 | tf_op jit(solution)/shard_map/ppermute | solution.py:57
  76.1 41.9 %collective-permute-start.16 = (bf16[1024,4,128]{2,1,0:T(4,128)(2,1)S(1)}, bf16[1024,4,128]{2,1,0:T(4,128)(2,1)S(1)}, u32[]{:S(2)}, u32[]{:S(2)}) collective-permute-start(bf16[1024,4,128]{2,1,0:T(4,128)(2,1)S(1)} %collective-permute-done.12.refs_2_), channel_id=1, source_target_pairs={{32,0},{33,1},{34,2},{35,3},{36,4},{37,5},{38,6},{39,7},{40,8},{41... | collective-permute-start | bytes 3145736 | tf_op jit(solution)/shard_map/ppermute | solution.py:57
  76.6 41.4 %collective-permute-start.15 = (bf16[1024,4,128]{2,1,0:T(4,128)(2,1)S(1)}, bf16[1024,4,128]{2,1,0:T(4,128)(2,1)S(1)}, u32[]{:S(2)}, u32[]{:S(2)}) collective-permute-start(bf16[1024,4,128]{2,1,0:T(4,128)(2,1)S(1)} %collective-permute-done.11.refs_1_), channel_id=1, source_target_pairs={{32,0},{33,1},{34,2},{35,3},{36,4},{37,5},{38,6},{39,7},{40,8},{41... | collective-permute-start | bytes 3145736 | tf_op jit(solution)/shard_map/ppermute | solution.py:57
  77.2 1.0 copy-start.3
  78.3 1.0 copy-start.5
  79.3 2.2 %copy-start.18 = (bf16[4096,512]{1,0:T(8,128)(2,1)S(1)}, bf16[4096,512]{1,0:T(8,128)(2,1)}, u32[]{:S(2)}) copy-start(bf16[4096,512]{1,0:T(8,128)(2,1)} %edges_ref.1) | copy-start | bytes 12582916
  81.5 1.0 copy-start.19
  82.6 1.0 copy-start.20
  83.6 1.0 copy-start.22
  84.6 35.3 %copy-start.4 = (bf16[512,512]{1,0:T(8,128)(2,1)S(1)}, bf16[512,512]{1,0:T(8,128)(2,1)}, u32[]{:S(2)}) copy-start(bf16[512,512]{1,0:T(8,128)(2,1)} %refs_15_.1) | copy-start | bytes 1572868
  84.6 35.3 %copy-start.6 = (bf16[512,512]{1,0:T(8,128)(2,1)S(1)}, bf16[512,512]{1,0:T(8,128)(2,1)}, u32[]{:S(2)}) copy-start(bf16[512,512]{1,0:T(8,128)(2,1)} %refs_16_.1) | copy-start | bytes 1572868
  84.6 35.3 %copy-start.7 = (bf16[512,512]{1,0:T(8,128)(2,1)S(1)}, bf16[512,512]{1,0:T(8,128)(2,1)}, u32[]{:S(2)}) copy-start(bf16[512,512]{1,0:T(8,128)(2,1)} %refs_20_.1) | copy-start | bytes 1572868
  84.6 35.3 %copy-start.8 = (bf16[512,512]{1,0:T(8,128)(2,1)S(1)}, bf16[512,512]{1,0:T(8,128)(2,1)}, u32[]{:S(2)}) copy-start(bf16[512,512]{1,0:T(8,128)(2,1)} %refs_21_.1) | copy-start | bytes 1572868
  84.6 35.3 %copy-start.9 = (bf16[512,512]{1,0:T(8,128)(2,1)S(1)}, bf16[512,512]{1,0:T(8,128)(2,1)}, u32[]{:S(2)}) copy-start(bf16[512,512]{1,0:T(8,128)(2,1)} %refs_23_.1) | copy-start | bytes 1572868
  84.7 35.3 %copy-start.14 = (f32[512]{0:T(512)S(1)}, f32[512]{0:T(512)}, u32[]{:S(2)}) copy-start(f32[512]{0:T(512)} %param.36) | copy-start | bytes 6148
  84.7 35.3 %copy-start.15 = (f32[512]{0:T(512)S(1)}, f32[512]{0:T(512)}, u32[]{:S(2)}) copy-start(f32[512]{0:T(512)} %param.38) | copy-start | bytes 6148
  84.7 35.3 %copy-start.16 = (f32[512]{0:T(512)S(1)}, f32[512]{0:T(512)}, u32[]{:S(2)}) copy-start(f32[512]{0:T(512)} %param.39) | copy-start | bytes 6148
  84.7 35.3 %copy-start.17 = (f32[512]{0:T(512)S(1)}, f32[512]{0:T(512)}, u32[]{:S(2)}) copy-start(f32[512]{0:T(512)} %param.40) | copy-start | bytes 6148
  114.9 2.1 %copy-start.1 = (bf16[4096,512]{1,0:T(8,128)(2,1)}, bf16[4096,512]{1,0:T(8,128)(2,1)S(1)}, u32[]{:S(2)}) copy-start(bf16[4096,512]{1,0:T(8,128)(2,1)S(1)} %get-tuple-element.19.refs_11_) | copy-start | bytes 12582916
  117.0 1.0 copy-start.2
  118.0 1.0 copy-start.25
  118.0 1.3 copy-start.26
  118.0 1.6 %copy-start.27 = (bf16[1024,4,128]{2,1,0:T(4,128)(2,1)}, bf16[1024,4,128]{2,1,0:T(4,128)(2,1)S(1)}, u32[]{:S(2)}) copy-start(bf16[1024,4,128]{2,1,0:T(4,128)(2,1)S(1)} %collective-permute-done.16.refs_6_) | copy-start | bytes 3145732
  118.0 1.9 %copy-start.28 = (bf16[1024,4,128]{2,1,0:T(4,128)(2,1)}, bf16[1024,4,128]{2,1,0:T(4,128)(2,1)S(1)}, u32[]{:S(2)}) copy-start(bf16[1024,4,128]{2,1,0:T(4,128)(2,1)S(1)} %collective-permute-done.15.refs_5_) | copy-start | bytes 3145732
